TPU v7x, 32 devices: a whole 2x2x4 slice. The times are simulated.
32 devices in a mesh: dp: 4 (over y, x), expert: 8 (over z, core).
Axes of the slice: x: 2, y: 2, z: 4, core: 2. Of those that a mesh axis runs over, the one named last changes fastest.
Arguments:
- tokens: bfloat16 [4096, 2048], P(('dp', 'expert')), may hold values from -6 to 6
- cotangent: bfloat16 [4096, 2048], P(('dp', 'expert')), may hold values from -6 to 6
- routes: int32 [4096, 2], P(('dp', 'expert')), may hold values from 0 to 7, as said below
- route_weights: float32 [4096, 2], P(('dp', 'expert')), may hold values from 0.1 to 1
- capacity: int32 [8], replicated, may hold values from 16 to 32, as said below
- w_in: bfloat16 [8, 2, 1408, 2048], P('expert', None, 'dp'), may hold values from -0.125 to 0.125
- w_down: bfloat16 [8, 1408, 2048], P('expert', 'dp'), may hold values from -0.15625 to 0.15625
Outputs:
- mixed: bfloat16 [4096, 2048], P(('dp', 'expert'))
- d_tokens: bfloat16 [4096, 2048], P(('dp', 'expert'))
- d_route_weights: float32 [4096, 2], P(('dp', 'expert'))
- d_w_in: bfloat16 [8, 2, 1408, 2048], P('expert', None, 'dp')
- d_w_down: bfloat16 [8, 1408, 2048], P('expert', 'dp')
Inputs may be any that keep to these rules, and one draw needn't show every extreme that they name: Each token names two different experts; in every block of 128 rows (one device's tokens) some expert whose capacity is 32 is named by 32 or more routes. Some expert has capacity 32.
All inputs are finite; a program needn't handle non-finite values.
Results may differ from a plain program's by a relative error of at most 0.013.
Values may be sent and summed in bfloat16 or wider, within the bound.
A program may use at most 128 MiB of HBM per device.

v0:
```python
import jax
import jax.numpy as jnp
from jax import lax
from jax.sharding import PartitionSpec as P


def expert_forward(inputs, weights_in, weights_down):
    gate_value = jnp.einsum(
        "gecd,ehd->gech", inputs, weights_in[:, 0], preferred_element_type=jnp.float32
    )
    up_value = jnp.einsum(
        "gecd,ehd->gech", inputs, weights_in[:, 1], preferred_element_type=jnp.float32
    )
    sig_gate = jax.nn.sigmoid(gate_value)
    act_gate = gate_value * sig_gate
    hidden = (act_gate * up_value).astype(jnp.bfloat16)
    partial_out = jnp.einsum(
        "gech,ehd->gecd", hidden, weights_down, preferred_element_type=jnp.float32
    )
    return ((gate_value, up_value, sig_gate, act_gate, hidden), partial_out)


def expert_backward(inputs, scaled, weights_in, weights_down, saved):
    gate_value, up_value, sig_gate, act_gate, hidden = saved
    hidden_grad = jnp.einsum(
        "gecd,ehd->gech", scaled, weights_down, preferred_element_type=jnp.float32
    )
    slope_gate = sig_gate * (1.0 + gate_value * (1.0 - sig_gate))
    gate_grad = (hidden_grad * up_value * slope_gate).astype(jnp.bfloat16)
    up_grad = (hidden_grad * act_gate).astype(jnp.bfloat16)
    gate_weight_grad = jnp.einsum(
        "gech,gecd->ehd", gate_grad, inputs, preferred_element_type=jnp.float32
    )
    up_weight_grad = jnp.einsum(
        "gech,gecd->ehd", up_grad, inputs, preferred_element_type=jnp.float32
    )
    down_weight_grad = jnp.einsum(
        "gech,gecd->ehd", hidden, scaled, preferred_element_type=jnp.float32
    )
    input_grad = jnp.einsum(
        "gech,ehd->gecd", gate_grad, weights_in[:, 0], preferred_element_type=jnp.float32
    )
    input_grad = input_grad + jnp.einsum(
        "gech,ehd->gecd", up_grad, weights_in[:, 1], preferred_element_type=jnp.float32
    )
    return (jnp.stack([gate_weight_grad, up_weight_grad], axis=1), down_weight_grad, input_grad)


def body(tokens, cotangent, routes, route_weights, capacity, w_in, w_down):
    experts = capacity.shape[0]
    expert_devs = lax.axis_size("expert")
    local_experts = experts // expert_devs
    tok_rows = tokens.shape[0]
    width = tokens.shape[1]
    slots = tok_rows * 2 // experts
    flat_expert = routes.reshape(-1)
    expert_ids = jnp.arange(experts, dtype=jnp.int32)
    onehot = (flat_expert[:, None] == expert_ids[None, :]).astype(jnp.int32)
    earlier = jnp.cumsum(onehot, axis=0) - onehot
    route_rank = jnp.sum(earlier * onehot, axis=1)
    cap_limit = jnp.sum(onehot * capacity[None, :], axis=1)
    kept_mask = route_rank < cap_limit
    dummy = experts * slots
    slot_target = jnp.where(kept_mask, flat_expert * slots + route_rank, dummy)
    route_count = 2 * tok_rows
    route_ids = jnp.arange(route_count, dtype=jnp.int32)
    slot_owner = (
        jnp.full((dummy + 1,), route_count, jnp.int32).at[slot_target].set(route_ids)[:dummy]
    )
    token_of = slot_owner // 2
    padded_tokens = jnp.concatenate([tokens, jnp.zeros((1, width), tokens.dtype)], axis=0)
    padded_cot = jnp.concatenate([cotangent, jnp.zeros((1, width), cotangent.dtype)], axis=0)
    padded_weights = jnp.concatenate(
        [route_weights.reshape(-1), jnp.zeros((1,), jnp.float32)], axis=0
    )
    bucket_shape = (expert_devs, local_experts, slots, width)
    send_inputs = padded_tokens[token_of].reshape(bucket_shape)
    send_scaled = (
        (padded_weights[slot_owner][:, None] * padded_cot[token_of].astype(jnp.float32))
        .astype(jnp.bfloat16)
        .reshape(bucket_shape)
    )
    recv_inputs = lax.all_to_all(send_inputs, "expert", split_axis=0, concat_axis=0, tiled=True)
    use_inputs = lax.all_gather(recv_inputs, "dp", axis=0, tiled=True)
    saved, partial_out = expert_forward(use_inputs, w_in, w_down)
    out_local = lax.psum_scatter(
        partial_out.astype(jnp.bfloat16), "dp", scatter_dimension=0, tiled=True
    )
    out_back = lax.all_to_all(out_local, "expert", split_axis=0, concat_axis=0, tiled=True)
    recv_scaled = lax.all_to_all(send_scaled, "expert", split_axis=0, concat_axis=0, tiled=True)
    use_scaled = lax.all_gather(recv_scaled, "dp", axis=0, tiled=True)
    in_weight_grad, down_weight_grad, input_grad = expert_backward(
        use_inputs, use_scaled, w_in, w_down, saved
    )
    grad_local = lax.psum_scatter(
        input_grad.astype(jnp.bfloat16), "dp", scatter_dimension=0, tiled=True
    )
    grad_back = lax.all_to_all(grad_local, "expert", split_axis=0, concat_axis=0, tiled=True)
    flat_out = jnp.concatenate(
        [out_back.reshape(dummy, width), jnp.zeros((1, width), jnp.bfloat16)], axis=0
    )
    flat_grad = jnp.concatenate(
        [grad_back.reshape(dummy, width), jnp.zeros((1, width), jnp.bfloat16)], axis=0
    )
    out_route = flat_out[slot_target].reshape(tok_rows, 2, width).astype(jnp.float32)
    grad_route = flat_grad[slot_target].reshape(tok_rows, 2, width).astype(jnp.float32)
    mixed = jnp.sum(route_weights[:, :, None] * out_route, axis=1).astype(jnp.bfloat16)
    d_route_weights = jnp.sum(out_route * cotangent.astype(jnp.float32)[:, None, :], axis=2)
    d_tokens = jnp.sum(grad_route, axis=1).astype(jnp.bfloat16)
    return (
        mixed,
        d_tokens,
        d_route_weights,
        in_weight_grad.astype(jnp.bfloat16),
        down_weight_grad.astype(jnp.bfloat16),
    )


def solution(mesh):
    placed = (
        P(("dp", "expert"), None),
        P(("dp", "expert"), None),
        P(("dp", "expert"), None),
        P(("dp", "expert"), None),
        P(),
        P("expert", None, "dp", None),
        P("expert", "dp", None),
    )
    return jax.shard_map(
        body,
        mesh=mesh,
        in_specs=placed,
        out_specs=(
            P(("dp", "expert"), None),
            P(("dp", "expert"), None),
            P(("dp", "expert"), None),
            P("expert", None, "dp", None),
            P("expert", "dp", None),
        ),
        check_vma=False,
    )
```

profile of v0, /device:TPU:0, one launch (start us, length us, event | category | flops | bytes accessed | tf_op | source)
XLA Modules:
  0.0 320.7 jit_solution(16261280849117789705)
XLA Ops:
  7.2 0.0 copy-start
  7.2 0.0 all-gather.3.cloned.1.call-start
  7.2 0.8 broadcast_multiply_fusion
  8.0 0.8 copy.31
  8.8 0.1 eq.29
  8.9 0.1 eq.25
  9.1 0.1 copy.33
  9.2 0.1 mul.91
  9.3 0.6 reduce-window.6
  9.9 0.2 slice_reduce_fusion
  10.2 0.8 select_reduce_fusion
  11.0 1.4 scatter_custom_fusion
  12.4 1.1 concatenate.24
  13.5 1.4 gather_fusion
  14.9 0.0 copy-start.9
  14.9 32.8 %all_to_all.20 = bf16[8,1,32,2048]{3,2,1,0:T(8,128)(2,1)} all-to-all(bf16[8,1,32,2048]{3,2,1,0:T(8,128)(2,1)S(1)} %bitcast.184), channel_id=1, replica_groups=mesh['dp'=4,'expert'=8] {'expert'}, dimensions={0} | all-to-all | bytes 2097152 | tf_op jit(solution)/shard_map/all_to_all | solution.py:83
  47.7 0.0 all-gather.3.cloned.1.call-update
  47.7 0.0 all-gather.5.cloned.1.call-start
  47.8 0.0 copy-done.9
  47.8 0.1 copy.30
  47.9 0.1 reshape.223
  48.1 1.9 gather_fusion.2
  50.0 0.1 mul.95
  50.1 0.0 copy-done.4
  50.1 1.4 gather_fusion.3
  51.5 0.2 fusion.40
  51.8 29.7 %all_to_all.21 = bf16[8,1,32,2048]{3,2,1,0:T(8,128)(2,1)} all-to-all(bf16[8,1,32,2048]{3,2,1,0:T(8,128)(2,1)S(1)} %fusion.40), channel_id=1, replica_groups=mesh['dp'=4,'expert'=8] {'expert'}, dimensions={0} | all-to-all | bytes 2097152 | tf_op jit(solution)/shard_map/all_to_all | solution.py:90
  81.5 0.0 all-gather.5.cloned.1.call-update
  81.5 0.0 reduce-scatter.3.cloned.1.call-start
  81.5 18.0 %all-gather.3.cloned.1.call-done = bf16[32,1,32,2048]{3,2,1,0:T(8,128)(2,1)} async-done(((bf16[8,1,32,2048]{3,2,1,0:T(8,128)(2,1)}), bf16[32,1,32,2048]{3,2,1,0:T(8,128)(2,1)}) %all-gather.3.cloned.1.call-update) | async-done | bytes 4194320 | tf_op jit(solution)/shard_map/all_gather | solution.py:84
  99.5 6.3 %fusion.8 = f32[32,32,352]{2,1,0:T(8,128)} fusion(bf16[32,1,32,2048]{3,2,1,0:T(8,128)(2,1)} %all-gather.3.cloned.1.call-done, bf16[1,2,352,2048]{3,2,1,0:T(8,128)(2,1)} %param.12), kind=kOutput, calls=%fused_computation.15 | convolution fusion | flops 1476395008 | bytes 7077888 | tf_op jit(solution)/shard_map/gecd,ehd->gech/dot_general | solution.py:11
  105.8 3.5 %fusion.10 = f32[32,32,352]{2,1,0:T(8,128)} fusion(bf16[32,1,32,2048]{3,2,1,0:T(8,128)(2,1)S(1)} %copy-done.10, bf16[1,2,352,2048]{3,2,1,0:T(8,128)(2,1)S(1)} %copy-done.2), kind=kOutput, calls=%fused_computation.17 | convolution fusion | flops 1476395008 | bytes 7077888 | tf_op jit(solution)/shard_map/gecd,ehd->gech/dot_general | solution.py:8
  109.3 44.7 %all-gather.5.cloned.1.call-done = bf16[32,1,32,2048]{3,2,1,0:T(8,128)(2,1)} async-done(((bf16[8,1,32,2048]{3,2,1,0:T(8,128)(2,1)}), bf16[32,1,32,2048]{3,2,1,0:T(8,128)(2,1)}) %all-gather.5.cloned.1.call-update) | async-done | bytes 4194320 | tf_op jit(solution)/shard_map/all_gather | solution.py:91
  154.1 5.9 %fusion.62 = (bf16[32,32,352]{2,1,0:T(8,128)(2,1)S(1)}, bf16[32,1,32,352]{3,2,0,1:T(8,128)(2,1)S(1)}, bf16[32,32,352]{2,1,0:T(8,128)(2,1)S(1)}) fusion(f32[32,32,352]{2,1,0:T(8,128)} %fusion.10, f32[32,32,352]{2,1,0:T(8,128)} %fusion.8, bf16[1,352,2048]{2,1,0:T(8,128)(2,1)S(1)} %copy-done, bf16[32,1,32,2048]{3,2,1,0:T(8,128)(2,1)} %all-gather.5.cloned.1.call-done), kind=kOutput, calls=%fused_computation.62 | convolution fusion | flops 1481801728 | bytes 10682368 | tf_op jit(solution)/shard_map/gecd,ehd->gech/dot_general | solution.py:25
  160.0 0.0 copy-start.6
  160.0 0.9 copy-done.13
  160.9 4.3 %convert_bitcast_fusion = bf16[32,1,32,2048]{3,2,0,1:T(8,128)(2,1)} fusion(bf16[32,32,352]{2,1,0:T(8,128)(2,1)S(1)} %get-tuple-element.16, bf16[1,352,2048]{2,1,0:T(8,128)(2,1)S(1)} %copy-done), kind=kOutput, calls=%fused_computation.19 | convolution fusion | flops 1478492160 | bytes 6356992 | tf_op jit(solution)/shard_map/gech,ehd->gecd/dot_general | solution.py:17
  165.2 0.0 reduce-scatter.3.cloned.1.call-update
  165.2 0.2 reduce-scatter.5.cloned.1.call-start
  165.4 0.0 copy-start.3
  165.4 3.8 %fusion.52 = f32[32,32,2048]{2,1,0:T(8,128)S(1)} fusion(bf16[1,2,352,2048]{3,2,1,0:T(8,128)(2,1)} %param.12, bf16[32,1,32,352]{3,2,0,1:T(8,128)(2,1)S(1)} %get-tuple-element.15), kind=kOutput, calls=%fused_computation.52 | convolution fusion | flops 1476395008 | bytes 10551296 | tf_op jit(solution)/shard_map/gech,ehd->gecd/dot_general | solution.py:40
  169.3 4.3 %fusion.12 = bf16[32,1,32,2048]{3,2,0,1:T(8,128)(2,1)} fusion(f32[32,32,2048]{2,1,0:T(8,128)S(1)} %fusion.52, bf16[32,32,352]{2,1,0:T(8,128)(2,1)S(1)} %get-tuple-element.14, bf16[1,2,352,2048]{3,2,1,0:T(8,128)(2,1)S(1)} %copy-done.3), kind=kOutput, calls=%fused_computation.20 | convolution fusion | flops 1480589312 | bytes 14811136 | tf_op jit(solution)/shard_map/gech,ehd->gecd/dot_general | solution.py:43
  173.6 0.0 reduce-scatter.5.cloned.1.call-update
  173.7 1.0 copy-done.5
  174.7 1.1 convert_element_type.115
  175.8 42.2 %reduce-scatter.3.cloned.1.call-done = bf16[8,1,32,2048]{3,2,0,1:T(8,128)(2,1)} async-done(((bf16[32,1,32,2048]{3,2,0,1:T(8,128)(2,1)}), bf16[8,1,32,2048]{3,2,0,1:T(8,128)(2,1)}) %reduce-scatter.3.cloned.1.call-update) | async-done | bytes 1048592 | tf_op jit(solution)/shard_map/reduce_scatter | solution.py:86
  218.0 4.6 %all-to-all-start.1 = ((bf16[8,1,32,2048]{3,2,1,0:T(8,128)(2,1)}), bf16[8,1,32,2048]{3,2,1,0:T(8,128)(2,1)S(1)}, u32[]{:S(2)}, u32[]{:S(2)}) async-start(bf16[8,1,32,2048]{3,2,1,0:T(8,128)(2,1)} %bitcast.187), calls=%async_computation.2 | async-start | bytes 2097152 | tf_op jit(solution)/shard_map/all_to_all | solution.py:89
  222.7 5.1 %fusion.34 = bf16[1,1,352,2048]{3,2,1,0:T(8,128)(2,1)} fusion(bf16[32,32,352]{2,1,0:T(8,128)(2,1)S(1)} %get-tuple-element.14, bf16[32,1,32,2048]{3,2,1,0:T(8,128)(2,1)} %all-gather.3.cloned.1.call-done), kind=kOutput, calls=%fused_computation.29 | convolution fusion | flops 1477115904 | bytes 6356992 | tf_op jit(solution)/shard_map/gech,gecd->ehd/dot_general | solution.py:34
  227.8 2.8 fusion.31
  230.6 43.2 %reduce-scatter.5.cloned.1.call-done = bf16[8,1,32,2048]{3,2,0,1:T(8,128)(2,1)} async-done(((bf16[32,1,32,2048]{3,2,0,1:T(8,128)(2,1)}), bf16[8,1,32,2048]{3,2,0,1:T(8,128)(2,1)}) %reduce-scatter.5.cloned.1.call-update) | async-done | bytes 1048592 | tf_op jit(solution)/shard_map/reduce_scatter | solution.py:95
  273.8 0.0 all-to-all-done.1
  273.9 4.6 %all-to-all-start.3 = ((bf16[8,1,32,2048]{3,2,1,0:T(8,128)(2,1)}), bf16[8,1,32,2048]{3,2,1,0:T(8,128)(2,1)}, u32[]{:S(2)}, u32[]{:S(2)}) async-start(bf16[8,1,32,2048]{3,2,1,0:T(8,128)(2,1)} %bitcast.186), calls=%async_computation.5 | async-start | bytes 2097152 | tf_op jit(solution)/shard_map/all_to_all | solution.py:98
  278.5 3.8 %pad_maximum_fusion = bf16[1,2,352,2048]{3,2,1,0:T(8,128)(2,1)} fusion(bf16[1,1,352,2048]{3,2,1,0:T(8,128)(2,1)} %fusion.34, bf16[1,1,352,2048]{3,2,1,0:T(8,128)(2,1)} %fusion.31), kind=kLoop, calls=%fused_computation.24 | loop fusion | flops 1441792 | bytes 5767168 | tf_op jit(solution)/shard_map/stack | solution.py:46
  282.3 2.8 fusion.37
  285.1 1.3 concatenate.25
  286.4 2.3 gather_fusion.1
  288.7 2.4 reshape.229
  291.1 6.0 %multiply_reduce_fusion = (f32[128,2]{1,0:T(8,128)}, bf16[128,2048]{1,0:T(8,128)(2,1)}) fusion(f32[128,2,2048]{2,1,0:T(2,128)S(1)} %reshape.229, f32[128,2048]{1,0:T(8,128)} %convert_element_type.115, f32[128,2]{1,0:T(8,128)} %copy-done.8), kind=kLoop, calls=%fused_computation.33 | loop fusion | flops 1834752 | bytes 3672064 | tf_op jit(solution)/shard_map/reduce_sum | solution.py:108
  297.0 1.5 copy.39
  298.5 6.7 %all-to-all-done.3 = bf16[8,1,32,2048]{3,2,1,0:T(8,128)(2,1)} async-done(((bf16[8,1,32,2048]{3,2,1,0:T(8,128)(2,1)}), bf16[8,1,32,2048]{3,2,1,0:T(8,128)(2,1)}, u32[]{:S(2)}, u32[]{:S(2)}) %all-to-all-start.3) | async-done | bytes 1048608 | tf_op jit(solution)/shard_map/all_to_all | solution.py:98
  305.2 1.3 concatenate.28
  306.5 2.3 gather_fusion.4
  308.8 1.7 reshape.228
  310.5 3.6 %reduce_sum.57 = bf16[128,2048]{1,0:T(8,128)(2,1)} reduce(bf16[128,2,2048]{2,1,0:T(2,128)(2,1)S(1)} %reshape.228, bf16[]{:T(256)} %constant.14.clone.1), dimensions={1}, to_apply=%region_8.9 | reduce | flops 262144 | bytes 1572866 | tf_op jit(solution)/shard_map/reduce_sum | solution.py:109
  (32 shorter events, 0.2 us)
Async XLA Ops:
  7.2 146.9 %copy-start = (bf16[1,352,2048]{2,1,0:T(8,128)(2,1)S(1)}, bf16[1,352,2048]{2,1,0:T(8,128)(2,1)}, u32[]{:S(2)}) copy-start(bf16[1,352,2048]{2,1,0:T(8,128)(2,1)} %param.13) | copy-start | bytes 4325380
  7.2 92.3 %all-gather.3.cloned.1.call-start = ((), (), s32[]{:S(2)}) async-start(), calls=%async_computation.6 | async-start | bytes 5242880 | tf_op jit(solution)/shard_map/all_gather | solution.py:84
  14.9 32.9 %copy-start.9 = (f32[128,2]{0,1:T(2,128)S(1)}, f32[128,2]{0,1:T(2,128)}, u32[]{:S(2)}) copy-start(f32[128,2]{0,1:T(2,128)} %param.10) | copy-start | bytes 3076
  47.7 2.4 copy-start.4
  47.7 106.3 %all-gather.5.cloned.1.call-start = ((), (), s32[]{:S(2)}) async-start(), calls=%async_computation.8 | async-start | bytes 5242880 | tf_op jit(solution)/shard_map/all_gather | solution.py:91
  47.9 2.2 copy-start.8
  81.5 136.5 %reduce-scatter.3.cloned.1.call-start = ((), (), s32[]{:S(2)}) async-start(), calls=%async_computation.7 | async-start | bytes 5242880 | tf_op jit(solution)/shard_map/reduce_scatter | solution.py:86
  99.5 6.3 %copy-start.2 = (bf16[1,2,352,2048]{3,2,1,0:T(8,128)(2,1)S(1)}, bf16[1,2,352,2048]{3,2,1,0:T(8,128)(2,1)}, u32[]{:S(2)}) copy-start(bf16[1,2,352,2048]{3,2,1,0:T(8,128)(2,1)} %param.12) | copy-start | bytes 8650756
  99.5 6.3 %copy-start.10 = (bf16[32,1,32,2048]{3,2,1,0:T(8,128)(2,1)S(1)}, bf16[32,1,32,2048]{3,2,1,0:T(8,128)(2,1)}, u32[]{:S(2)}) copy-start(bf16[32,1,32,2048]{3,2,1,0:T(8,128)(2,1)} %all-gather.3.cloned.1.call-done) | copy-start | bytes 12582916
  160.0 0.9 copy-start.13
  160.0 5.4 %copy-start.6 = (bf16[32,1,32,352]{3,2,0,1:T(8,128)(2,1)}, bf16[32,1,32,352]{3,2,0,1:T(8,128)(2,1)S(1)}, u32[]{:S(2)}) copy-start(bf16[32,1,32,352]{3,2,0,1:T(8,128)(2,1)S(1)} %get-tuple-element.15) | copy-start | bytes 2162692
  165.2 108.7 %reduce-scatter.5.cloned.1.call-start = ((), (), s32[]{:S(2)}) async-start(), calls=%async_computation.9 | async-start | bytes 5242880 | tf_op jit(solution)/shard_map/reduce_scatter | solution.py:95
  165.4 3.9 %copy-start.3 = (bf16[1,2,352,2048]{3,2,1,0:T(8,128)(2,1)S(1)}, bf16[1,2,352,2048]{3,2,1,0:T(8,128)(2,1)}, u32[]{:S(2)}) copy-start(bf16[1,2,352,2048]{3,2,1,0:T(8,128)(2,1)} %param.12) | copy-start | bytes 8650756
  173.6 1.0 copy-start.5
  218.0 55.8 %all-to-all-start.1 = ((bf16[8,1,32,2048]{3,2,1,0:T(8,128)(2,1)}), bf16[8,1,32,2048]{3,2,1,0:T(8,128)(2,1)S(1)}, u32[]{:S(2)}, u32[]{:S(2)}) async-start(bf16[8,1,32,2048]{3,2,1,0:T(8,128)(2,1)} %bitcast.187), calls=%async_computation.2 | async-start | bytes 2097152 | tf_op jit(solution)/shard_map/all_to_all | solution.py:89
  222.6 5.1 %copy-start.7 = (bf16[32,1,32,352]{3,2,0,1:T(8,128)(2,1)S(1)}, bf16[32,1,32,352]{3,2,0,1:T(8,128)(2,1)}, u32[]{:S(2)}) copy-start(bf16[32,1,32,352]{3,2,0,1:T(8,128)(2,1)} %copy-done.6) | copy-start | bytes 2162692
  222.7 5.1 %copy-start.11 = (bf16[32,1,32,2048]{3,2,1,0:T(8,128)(2,1)S(1)}, bf16[32,1,32,2048]{3,2,1,0:T(8,128)(2,1)}, u32[]{:S(2)}) copy-start(bf16[32,1,32,2048]{3,2,1,0:T(8,128)(2,1)} %all-gather.3.cloned.1.call-done) | copy-start | bytes 12582916
  273.9 8.4 %copy-start.1 = (bf16[8,1,32,2048]{3,2,1,0:T(8,128)(2,1)}, bf16[8,1,32,2048]{3,2,1,0:T(8,128)(2,1)S(1)}, u32[]{:S(2)}) copy-start(bf16[8,1,32,2048]{3,2,1,0:T(8,128)(2,1)S(1)} %all-to-all-done.1) | copy-start | bytes 3145732
  273.9 31.3 %all-to-all-start.3 = ((bf16[8,1,32,2048]{3,2,1,0:T(8,128)(2,1)}), bf16[8,1,32,2048]{3,2,1,0:T(8,128)(2,1)}, u32[]{:S(2)}, u32[]{:S(2)}) async-start(bf16[8,1,32,2048]{3,2,1,0:T(8,128)(2,1)} %bitcast.186), calls=%async_computation.5 | async-start | bytes 2097152 | tf_op jit(solution)/shard_map/all_to_all | solution.py:98
  278.5 3.8 %copy-start.12 = (bf16[32,1,32,2048]{3,2,1,0:T(8,128)(2,1)S(1)}, bf16[32,1,32,2048]{3,2,1,0:T(8,128)(2,1)}, u32[]{:S(2)}) copy-start(bf16[32,1,32,2048]{3,2,1,0:T(8,128)(2,1)} %all-gather.5.cloned.1.call-done) | copy-start | bytes 12582916
  278.5 3.8 %copy-start.14 = (bf16[32,32,352]{2,1,0:T(8,128)(2,1)S(1)}, bf16[32,32,352]{2,1,0:T(8,128)(2,1)}, u32[]{:S(2)}) copy-start(bf16[32,32,352]{2,1,0:T(8,128)(2,1)} %copy-done.13) | copy-start | bytes 2162692
Sparse Core Ops, SparseCore 0:
  47.8 51.5 all-gather.2
  101.3 52.6 all-gather.4
  165.3 52.6 reduce-scatter.2
  221.1 52.6 reduce-scatter.4
where the time goes:
time: 321 us
  waiting for transfers between devices  155 us (48%)
  blocking collectives  62.5 us (19%)
  matrix products  39 us (12%)
  local copies, waits for them, and re-layouts  23.8 us (7%)
  other arithmetic  16.9 us (5%)
  between operations  14 us (4%)
  starting transfers between devices  9.58 us (3%)
    all_gather x1, waiting for transfers between devices, body(): use_scaled = lax.all_gather(recv_scaled, 'dp', axis=0, tiled=True)  44.7 us
    reduce_scatter x1, waiting for transfers between devices, body(): lax.psum_scatter(input_grad.astype(jnp.bfloat16), 'dp', scatter_dimension...  43.2 us
    reduce_scatter x1, waiting for transfers between devices, body(): lax.psum_scatter(partial_out.astype(jnp.bfloat16), 'dp', scatter_dimensio...  42.2 us
    all_to_all x1, blocking collectives, body(): lax.all_to_all(send_inputs, 'expert', split_axis=0, concat_axis=0, tiled=...  32.8 us
    all_to_all x1, blocking collectives, body(): lax.all_to_all(send_scaled, 'expert', split_axis=0, concat_axis=0, tiled=...  29.7 us
    all_gather x1, waiting for transfers between devices, body(): use_inputs = lax.all_gather(recv_inputs, 'dp', axis=0, tiled=True)  18 us
    all_to_all x1, waiting for transfers between devices, body(): lax.all_to_all(grad_local, 'expert', split_axis=0, concat_axis=0, tiled=T...  6.66 us
  transfers between devices with their start and end apart: 6, of which 5 were waited for; matrix products, arithmetic and copies ran while one was open for 16% of the time, Pallas kernels for 0%

commit v1 on v0

--- a/solution.py
+++ b/solution.py
@@ -88,7 +88,12 @@
     )
     out_back = lax.all_to_all(out_local, "expert", split_axis=0, concat_axis=0, tiled=True)
     recv_scaled = lax.all_to_all(send_scaled, "expert", split_axis=0, concat_axis=0, tiled=True)
-    use_scaled = lax.all_gather(recv_scaled, "dp", axis=0, tiled=True)
+    ring = [recv_scaled]
+    for hop in range(3):
+        ring.append(lax.ppermute(ring[-1], "dp", [(dev, (dev + 1) % 4) for dev in range(4)]))
+    use_scaled = jnp.roll(
+        jnp.concatenate(ring[::-1], axis=0), (lax.axis_index("dp") + 1) * ring[0].shape[0], axis=0
+    )
     in_weight_grad, down_weight_grad, input_grad = expert_backward(
         use_inputs, use_scaled, w_in, w_down, saved
     )

time: 321 us -> 367 us (1.14)
  waiting for transfers between devices: 155 us -> 241 us
  blocking collectives: 62.5 us -> 0 us
  starting transfers between devices: 9.58 us -> 23.3 us
  local copies, waits for them, and re-layouts: 23.8 us -> 35 us
    ppermute x0 -> x3, waiting for transfers between devices: none -> 91.2 us  [body(): lax.ppermute(ring[-1], 'dp', [(dev, (dev + 1) % 4) for dev in range(4)])]
    all_to_all x2 -> x0, blocking collectives: 62.5 us -> none  [the longest x1 32.8 us: body(): lax.all_to_all(send_inputs, 'expert', split_axis=0, concat_axis=0, tiled=...]
    all_to_all x0 -> x2, waiting for transfers between devices: none -> 45.8 us  [the longest x1 25.7 us: body(): lax.all_to_all(send_scaled, 'expert', split_axis=0, concat_axis=0, tiled=...]
    all_gather x1 -> x0, waiting for transfers between devices: 44.7 us -> none  [body(): use_scaled = lax.all_gather(recv_scaled, 'dp', axis=0, tiled=True)]
    all_gather x1, waiting for transfers between devices: 18 us -> 0.01 us  [body(): use_inputs = lax.all_gather(recv_inputs, 'dp', axis=0, tiled=True)]
    unnamed x33 -> x32, local copies, waits for them, and re-layouts: 4.31 us -> 15.6 us
    all_to_all x1, waiting for transfers between devices: 0.01 us -> 9.97 us  [body(): lax.all_to_all(out_local, 'expert', split_axis=0, concat_axis=0, tiled=True)]
    all_to_all x0 -> x2, starting transfers between devices: none -> 9.88 us  [the longest x1 6.33 us: body(): lax.all_to_all(send_inputs, 'expert', split_axis=0, concat_axis=0, tiled=...]
  transfers between devices with their start and end apart: 6 -> 10, of which waited for: 5 -> 8; matrix products, arithmetic and copies ran while one was open for 16% -> 12% of each run, Pallas kernels for 0% -> 0%
where the time goes in v1:
time: 367 us; the launch traced here: 366 us
  waiting for transfers between devices  241 us (66%)
  matrix products  36.6 us (10%)
  local copies, waits for them, and re-layouts  35 us (10%)
  starting transfers between devices  23.3 us (6%)
  other arithmetic  15.8 us (4%)
  between operations  14 us (4%)
    ppermute x3, waiting for transfers between devices, body(): lax.ppermute(ring[-1], 'dp', [(dev, (dev + 1) % 4) for dev in range(4)])  91.2 us
    reduce_scatter x1, waiting for transfers between devices, body(): lax.psum_scatter(input_grad.astype(jnp.bfloat16), 'dp', scatter_dimension...  47.4 us
    reduce_scatter x1, waiting for transfers between devices, body(): lax.psum_scatter(partial_out.astype(jnp.bfloat16), 'dp', scatter_dimensio...  46.2 us
    all_to_all x1, waiting for transfers between devices, body(): lax.all_to_all(send_scaled, 'expert', split_axis=0, concat_axis=0, tiled=...  25.7 us
    all_to_all x1, waiting for transfers between devices, body(): lax.all_to_all(send_inputs, 'expert', split_axis=0, concat_axis=0, tiled=...  20.1 us
    unnamed x32, local copies, waits for them, and re-layouts  15.6 us
    all_to_all x1, waiting for transfers between devices, body(): lax.all_to_all(out_local, 'expert', split_axis=0, concat_axis=0, tiled=True)  9.97 us
  transfers between devices with their start and end apart: 10, of which 8 were waited for; matrix products, arithmetic and copies ran while one was open for 12% of the time, Pallas kernels for 0%

profile of v1, /device:TPU:0, one launch (start us, length us, event | category | flops | bytes accessed | tf_op | source)
XLA Modules:
  0.0 366.1 jit_solution(636159580850233496)
XLA Ops:
  7.2 0.9 copy.31
  8.1 0.1 eq.32
  8.2 0.1 eq.28
  8.4 0.7 broadcast_multiply_fusion
  9.1 0.6 reduce-window.6
  9.6 0.2 slice_reduce_fusion
  9.9 0.1 copy.33
  10.0 0.1 mul.94
  10.1 0.7 select_reduce_fusion
  10.9 1.4 scatter_custom_fusion
  12.3 1.1 concatenate.30
  13.4 2.3 gather_fusion
  15.8 6.3 %all-to-all-start = ((bf16[8,1,32,2048]{3,2,1,0:T(8,128)(2,1)}), bf16[8,1,32,2048]{3,2,1,0:T(8,128)(2,1)}, u32[]{:S(2)}, u32[]{:S(2)}) async-start(bf16[8,1,32,2048]{3,2,1,0:T(8,128)(2,1)} %bitcast.6), calls=%async_computation | async-start | bytes 2097152 | tf_op jit(solution)/shard_map/all_to_all | solution.py:83
  22.1 1.1 concatenate.33
  23.2 1.4 gather_fusion.3
  24.6 0.1 copy.30
  24.7 0.6 copy-done.6
  25.3 0.1 reshape.223
  25.5 1.9 gather_fusion.2
  27.4 0.1 mul.98
  27.5 1.2 fusion.42
  28.7 20.1 %all-to-all-done = bf16[8,1,32,2048]{3,2,1,0:T(8,128)(2,1)} async-done(((bf16[8,1,32,2048]{3,2,1,0:T(8,128)(2,1)}), bf16[8,1,32,2048]{3,2,1,0:T(8,128)(2,1)}, u32[]{:S(2)}, u32[]{:S(2)}) %all-to-all-start) | async-done | bytes 1048608 | tf_op jit(solution)/shard_map/all_to_all | solution.py:83
  48.8 3.6 all-to-all-start.2
  52.4 0.7 all-gather.2.cloned.1.call-update
  53.1 25.7 %all-to-all-done.2 = bf16[8,1,32,2048]{3,2,1,0:T(8,128)(2,1)S(1)} async-done(((bf16[8,1,32,2048]{3,2,1,0:T(8,128)(2,1)}), bf16[8,1,32,2048]{3,2,1,0:T(8,128)(2,1)S(1)}, u32[]{:S(2)}, u32[]{:S(2)}) %all-to-all-start.2) | async-done | bytes 1048608 | tf_op jit(solution)/shard_map/all_to_all | solution.py:90
  78.9 1.5 collective-permute-start
  80.4 42.7 %collective-permute-done = bf16[8,1,32,2048]{3,2,1,0:T(8,128)(2,1)S(1)} collective-permute-done((bf16[8,1,32,2048]{3,2,1,0:T(8,128)(2,1)S(1)}, bf16[8,1,32,2048]{3,2,1,0:T(8,128)(2,1)S(1)}, u32[]{:S(2)}, u32[]{:S(2)}) %collective-permute-start) | collective-permute-done | bytes 1048608 | tf_op jit(solution)/shard_map/ppermute | solution.py:93
  123.1 2.0 collective-permute-start.1
  125.1 24.4 %collective-permute-done.1 = bf16[8,1,32,2048]{3,2,1,0:T(8,128)(2,1)} collective-permute-done((bf16[8,1,32,2048]{3,2,1,0:T(8,128)(2,1)S(1)}, bf16[8,1,32,2048]{3,2,1,0:T(8,128)(2,1)}, u32[]{:S(2)}, u32[]{:S(2)}) %collective-permute-start.1) | collective-permute-done | bytes 1048608 | tf_op jit(solution)/shard_map/ppermute | solution.py:93
  149.5 0.6 collective-permute-start.2
  150.1 24.1 %collective-permute-done.2 = bf16[8,1,32,2048]{3,2,1,0:T(8,128)(2,1)} collective-permute-done((bf16[8,1,32,2048]{3,2,1,0:T(8,128)(2,1)}, bf16[8,1,32,2048]{3,2,1,0:T(8,128)(2,1)}, u32[]{:S(2)}, u32[]{:S(2)}) %collective-permute-start.2) | collective-permute-done | bytes 1048608 | tf_op jit(solution)/shard_map/ppermute | solution.py:93
  174.2 2.3 constant_dynamic-update-slice_fusion.7
  176.5 2.3 constant_dynamic-update-slice_fusion.6
  178.9 1.1 constant_dynamic-update-slice_fusion.5
  180.0 1.0 constant_dynamic-update-slice_fusion.4
  181.0 2.3 constant_dynamic-update-slice_fusion.3
  183.3 2.3 constant_dynamic-update-slice_fusion.2
  185.7 1.1 constant_dynamic-update-slice_fusion.1
  186.7 1.1 constant_dynamic-update-slice_fusion
  187.8 5.1 %fusion.10 = f32[32,32,352]{2,1,0:T(8,128)S(1)} fusion(bf16[32,1,32,2048]{3,2,1,0:T(8,128)(2,1)} %all-gather.2.cloned.1.call-done, bf16[1,2,352,2048]{3,2,1,0:T(8,128)(2,1)} %param.12), kind=kOutput, calls=%fused_computation.17 | convolution fusion | flops 1476395008 | bytes 7077888 | tf_op jit(solution)/shard_map/gecd,ehd->gech/dot_general | solution.py:8
  192.9 2.3 fusion.8
  195.3 5.1 %fusion.64 = (bf16[32,32,352]{2,1,0:T(8,128)(2,1)S(1)}, bf16[32,1,32,352]{3,2,0,1:T(8,128)(2,1)S(1)}, bf16[32,32,352]{2,1,0:T(8,128)(2,1)S(1)}) fusion(f32[32,32,352]{2,1,0:T(8,128)S(1)} %fusion.10, f32[32,32,352]{2,1,0:T(8,128)S(1)} %fusion.8, bf16[1,352,2048]{2,1,0:T(8,128)(2,1)S(1)} %copy-done, ...), kind=kOutput, calls=%fused_computation.64 | convolution fusion | flops 1481801728 | bytes 10682372 | tf_op jit(solution)/shard_map/gecd,ehd->gech/dot_general | solution.py:25
  200.4 2.3 fusion.54
  202.8 4.3 %fusion.14 = bf16[32,1,32,2048]{3,2,0,1:T(8,128)(2,1)} fusion(f32[32,32,2048]{2,1,0:T(8,128)S(1)} %fusion.54, bf16[32,32,352]{2,1,0:T(8,128)(2,1)S(1)} %get-tuple-element.14, bf16[1,2,352,2048]{3,2,1,0:T(8,128)(2,1)S(1)} %copy-done.2), kind=kOutput, calls=%fused_computation.22 | convolution fusion | flops 1480589312 | bytes 14811136 | tf_op jit(solution)/shard_map/gech,ehd->gecd/dot_general | solution.py:43
  207.1 4.3 %convert_bitcast_fusion = bf16[32,1,32,2048]{3,2,0,1:T(8,128)(2,1)} fusion(bf16[32,32,352]{2,1,0:T(8,128)(2,1)S(1)} %get-tuple-element.16, bf16[1,352,2048]{2,1,0:T(8,128)(2,1)S(1)} %copy-done), kind=kOutput, calls=%fused_computation.19 | convolution fusion | flops 1478492160 | bytes 6356992 | tf_op jit(solution)/shard_map/gech,ehd->gecd/dot_general | solution.py:17
  211.4 47.4 %reduce-scatter.5.cloned.1.call-done = bf16[8,1,32,2048]{3,2,0,1:T(8,128)(2,1)} async-done(((bf16[32,1,32,2048]{3,2,0,1:T(8,128)(2,1)}), bf16[8,1,32,2048]{3,2,0,1:T(8,128)(2,1)}) %reduce-scatter.5.cloned.1.call-update) | async-done | bytes 1048592 | tf_op jit(solution)/shard_map/reduce_scatter | solution.py:100
  258.8 4.6 %all-to-all-start.3 = ((bf16[8,1,32,2048]{3,2,1,0:T(8,128)(2,1)}), bf16[8,1,32,2048]{3,2,1,0:T(8,128)(2,1)S(1)}, u32[]{:S(2)}, u32[]{:S(2)}) async-start(bf16[8,1,32,2048]{3,2,1,0:T(8,128)(2,1)} %bitcast.185), calls=%async_computation.5 | async-start | bytes 2097152 | tf_op jit(solution)/shard_map/all_to_all | solution.py:103
  263.4 1.1 convert_element_type.115
  264.5 4.1 %fusion.36 = bf16[1,1,352,2048]{3,2,1,0:T(8,128)(2,1)S(1)} fusion(bf16[32,1,32,2048]{3,2,1,0:T(8,128)(2,1)} %all-gather.2.cloned.1.call-done, bf16[32,1,32,352]{3,2,0,1:T(8,128)(2,1)} %copy-done.5), kind=kOutput, calls=%fused_computation.31 | convolution fusion | flops 1477115904 | bytes 6356992 | tf_op jit(solution)/shard_map/gech,gecd->ehd/dot_general | solution.py:31
  268.6 46.2 %reduce-scatter.3.cloned.1.call-done = bf16[8,1,32,2048]{3,2,0,1:T(8,128)(2,1)} async-done(((bf16[32,1,32,2048]{3,2,0,1:T(8,128)(2,1)}), bf16[8,1,32,2048]{3,2,0,1:T(8,128)(2,1)}) %reduce-scatter.3.cloned.1.call-update) | async-done | bytes 1048592 | tf_op jit(solution)/shard_map/reduce_scatter | solution.py:86
  314.8 4.6 %all-to-all-start.1 = ((bf16[8,1,32,2048]{3,2,1,0:T(8,128)(2,1)}), bf16[8,1,32,2048]{3,2,1,0:T(8,128)(2,1)}, u32[]{:S(2)}, u32[]{:S(2)}) async-start(bf16[8,1,32,2048]{3,2,1,0:T(8,128)(2,1)} %bitcast.184), calls=%async_computation.2 | async-start | bytes 2097152 | tf_op jit(solution)/shard_map/all_to_all | solution.py:89
  319.4 4.1 %fusion.39 = bf16[1,1,352,2048]{3,2,1,0:T(8,128)(2,1)S(1)} fusion(bf16[32,32,352]{2,1,0:T(8,128)(2,1)} %copy-done.4, bf16[32,1,32,2048]{3,2,1,0:T(8,128)(2,1)} %all-gather.2.cloned.1.call-done), kind=kOutput, calls=%fused_computation.32 | convolution fusion | flops 1477115904 | bytes 6356992 | tf_op jit(solution)/shard_map/gech,gecd->ehd/dot_general | solution.py:34
  323.5 1.8 pad_maximum_fusion
  325.3 5.0 %fusion.33 = bf16[1,352,2048]{2,1,0:T(8,128)(2,1)} fusion(bf16[32,32,352]{2,1,0:T(8,128)(2,1)S(1)} %copy-done.10, bf16[64,1,32,2048]{3,2,1,0:T(8,128)(2,1)} %constant_dynamic-update-slice_fusion, s32[]{:T(128)S(6)} %select_n.54), kind=kOutput, calls=%fused_computation.30 | convolution fusion | flops 1477115904 | bytes 6356996 | tf_op jit(solution)/shard_map/gech,gecd->ehd/dot_general | solution.py:37
  330.3 0.1 concatenate.35
  330.4 1.4 gather_fusion.4
  331.8 0.7 reshape.228
  332.5 3.6 reduce_sum.57
  336.1 10.0 %all-to-all-done.1 = bf16[8,1,32,2048]{3,2,1,0:T(8,128)(2,1)} async-done(((bf16[8,1,32,2048]{3,2,1,0:T(8,128)(2,1)}), bf16[8,1,32,2048]{3,2,1,0:T(8,128)(2,1)}, u32[]{:S(2)}, u32[]{:S(2)}) %all-to-all-start.1) | async-done | bytes 1048608 | tf_op jit(solution)/shard_map/all_to_all | solution.py:89
  346.1 1.3 concatenate.31
  347.4 2.3 gather_fusion.1
  349.7 2.4 reshape.229
  352.1 6.0 %multiply_reduce_fusion = (f32[128,2]{1,0:T(8,128)}, bf16[128,2048]{1,0:T(8,128)(2,1)}) fusion(f32[128,2,2048]{2,1,0:T(2,128)S(1)} %reshape.229, f32[128,2048]{1,0:T(8,128)} %convert_element_type.115, f32[128,2]{1,0:T(8,128)} %copy-done.6), kind=kLoop, calls=%fused_computation.35 | loop fusion | flops 1834752 | bytes 3672064 | tf_op jit(solution)/shard_map/reduce_sum | solution.py:113
  358.1 1.5 copy.39
  (37 shorter events, 0.3 us)
Async XLA Ops:
  7.2 188.1 %copy-start = (bf16[1,352,2048]{2,1,0:T(8,128)(2,1)S(1)}, bf16[1,352,2048]{2,1,0:T(8,128)(2,1)}, u32[]{:S(2)}) copy-start(bf16[1,352,2048]{2,1,0:T(8,128)(2,1)} %param.13) | copy-start | bytes 4325380
  15.8 33.0 %all-to-all-start = ((bf16[8,1,32,2048]{3,2,1,0:T(8,128)(2,1)}), bf16[8,1,32,2048]{3,2,1,0:T(8,128)(2,1)}, u32[]{:S(2)}, u32[]{:S(2)}) async-start(bf16[8,1,32,2048]{3,2,1,0:T(8,128)(2,1)} %bitcast.6), calls=%async_computation | async-start | bytes 2097152 | tf_op jit(solution)/shard_map/all_to_all | solution.py:83
  23.2 1.4 copy-start.7
  24.7 0.6 copy-start.6
  48.8 30.1 %all-to-all-start.2 = ((bf16[8,1,32,2048]{3,2,1,0:T(8,128)(2,1)}), bf16[8,1,32,2048]{3,2,1,0:T(8,128)(2,1)S(1)}, u32[]{:S(2)}, u32[]{:S(2)}) async-start(bf16[8,1,32,2048]{3,2,1,0:T(8,128)(2,1)} %fusion.42), calls=%async_computation.3 | async-start | bytes 2097152 | tf_op jit(solution)/shard_map/all_to_all | solution.py:90
  52.4 135.4 %all-gather.2.cloned.1.call-start = ((), (), s32[]{:S(2)}) async-start(), calls=%async_computation.6 | async-start | bytes 5242880 | tf_op jit(solution)/shard_map/all_gather | solution.py:84
  53.1 205.7 %reduce-scatter.5.cloned.1.call-start = ((), (), s32[]{:S(2)}) async-start(), calls=%async_computation.8 | async-start | bytes 5242880 | tf_op jit(solution)/shard_map/reduce_scatter | solution.py:100
  78.9 44.2 %collective-permute-start = (bf16[8,1,32,2048]{3,2,1,0:T(8,128)(2,1)S(1)}, bf16[8,1,32,2048]{3,2,1,0:T(8,128)(2,1)S(1)}, u32[]{:S(2)}, u32[]{:S(2)}) collective-permute-start(bf16[8,1,32,2048]{3,2,1,0:T(8,128)(2,1)S(1)} %all-to-all-done.2), channel_id=1, source_target_pairs={{0,8},{8,16},{16,24},{24,0},{1,9},{9,17},{17,25},{25,1},{2,10},{10... | collective-permute-start | bytes 3145736 | tf_op jit(solution)/shard_map/ppermute | solution.py:93
  123.1 26.4 %collective-permute-start.1 = (bf16[8,1,32,2048]{3,2,1,0:T(8,128)(2,1)S(1)}, bf16[8,1,32,2048]{3,2,1,0:T(8,128)(2,1)}, u32[]{:S(2)}, u32[]{:S(2)}) collective-permute-start(bf16[8,1,32,2048]{3,2,1,0:T(8,128)(2,1)S(1)} %collective-permute-done), channel_id=1, source_target_pairs={{0,8},{8,16},{16,24},{24,0},{1,9},{9,17},{17,25},{25,1},{2,10},{10... | collective-permute-start | bytes 3145736 | tf_op jit(solution)/shard_map/ppermute | solution.py:93
  149.5 24.7 %collective-permute-start.2 = (bf16[8,1,32,2048]{3,2,1,0:T(8,128)(2,1)}, bf16[8,1,32,2048]{3,2,1,0:T(8,128)(2,1)}, u32[]{:S(2)}, u32[]{:S(2)}) collective-permute-start(bf16[8,1,32,2048]{3,2,1,0:T(8,128)(2,1)} %collective-permute-done.1), channel_id=1, source_target_pairs={{0,8},{8,16},{16,24},{24,0},{1,9},{9,17},{17,25},{25,1},{2,10},{10... | collective-permute-start | bytes 3145736 | tf_op jit(solution)/shard_map/ppermute | solution.py:93
  187.8 5.1 %copy-start.2 = (bf16[1,2,352,2048]{3,2,1,0:T(8,128)(2,1)S(1)}, bf16[1,2,352,2048]{3,2,1,0:T(8,128)(2,1)}, u32[]{:S(2)}) copy-start(bf16[1,2,352,2048]{3,2,1,0:T(8,128)(2,1)} %param.12) | copy-start | bytes 8650756
  187.8 5.1 %copy-start.8 = (bf16[32,1,32,2048]{3,2,1,0:T(8,128)(2,1)S(1)}, bf16[32,1,32,2048]{3,2,1,0:T(8,128)(2,1)}, u32[]{:S(2)}) copy-start(bf16[32,1,32,2048]{3,2,1,0:T(8,128)(2,1)} %all-gather.2.cloned.1.call-done) | copy-start | bytes 12582916
  200.4 2.4 copy-start.5
  200.4 2.4 copy-start.4
  200.4 6.7 %copy-start.9 = (bf16[32,32,352]{2,1,0:T(8,128)(2,1)}, bf16[32,32,352]{2,1,0:T(8,128)(2,1)S(1)}, u32[]{:S(2)}) copy-start(bf16[32,32,352]{2,1,0:T(8,128)(2,1)S(1)} %get-tuple-element.16) | copy-start | bytes 2162692
  207.1 107.7 %reduce-scatter.3.cloned.1.call-start = ((), (), s32[]{:S(2)}) async-start(), calls=%async_computation.7 | async-start | bytes 5242880 | tf_op jit(solution)/shard_map/reduce_scatter | solution.py:86
  211.4 52.0 %copy-start.3 = (bf16[128,2048]{1,0:T(8,128)(2,1)S(1)}, bf16[128,2048]{1,0:T(8,128)(2,1)}, u32[]{:S(2)}) copy-start(bf16[128,2048]{1,0:T(8,128)(2,1)} %param.8) | copy-start | bytes 1572868
  258.8 56.0 %all-to-all-start.3 = ((bf16[8,1,32,2048]{3,2,1,0:T(8,128)(2,1)}), bf16[8,1,32,2048]{3,2,1,0:T(8,128)(2,1)S(1)}, u32[]{:S(2)}, u32[]{:S(2)}) async-start(bf16[8,1,32,2048]{3,2,1,0:T(8,128)(2,1)} %bitcast.185), calls=%async_computation.5 | async-start | bytes 2097152 | tf_op jit(solution)/shard_map/all_to_all | solution.py:103
  314.8 31.3 %all-to-all-start.1 = ((bf16[8,1,32,2048]{3,2,1,0:T(8,128)(2,1)}), bf16[8,1,32,2048]{3,2,1,0:T(8,128)(2,1)}, u32[]{:S(2)}, u32[]{:S(2)}) async-start(bf16[8,1,32,2048]{3,2,1,0:T(8,128)(2,1)} %bitcast.184), calls=%async_computation.2 | async-start | bytes 2097152 | tf_op jit(solution)/shard_map/all_to_all | solution.py:89
  323.5 1.8 copy-start.10
  347.4 12.1 %copy-start.1 = (bf16[1,352,2048]{2,1,0:T(8,128)(2,1)S(1)}, bf16[1,352,2048]{2,1,0:T(8,128)(2,1)}, u32[]{:S(2)}) copy-start(bf16[1,352,2048]{2,1,0:T(8,128)(2,1)} %param.13) | copy-start | bytes 4325380
Sparse Core Ops, SparseCore 0:
  55.0 74.9 all-gather.1
  207.2 51.5 reduce-scatter.4
  262.1 52.6 reduce-scatter.2
